TPU v7x, 256 devices: a whole 4x4x8 slice. The times are simulated.
256 devices in a mesh: blk: 32 (over z, x), head: 2 (over core), rep: 4 (over y).
Axes of the slice: x: 4, y: 4, z: 8, core: 2. Of those that a mesh axis runs over, the one named last changes fastest.
Arguments:
- queries: bfloat16 [4096, 4096], P(('rep', 'blk'), 'head'), parts along dimension 0, may hold values from -400 to 400
- cache_keys: bfloat16 [131072, 256], P(('rep', 'blk'), 'head'), parts along dimension 0, may hold values from -6 to 6
- cache_values: bfloat16 [131072, 256], P(('rep', 'blk'), 'head'), parts along dimension 0, may hold values from -6 to 6
- slot_request: int32 [131072], P(('rep', 'blk')), parts along dimension 0, may hold values from 0 to 1, as said below
- slot_position: int32 [131072], P(('rep', 'blk')), parts along dimension 0, may hold values from 0 to 16383
- lengths: int32 [8], P('rep'), parts along dimension 0, may hold values from 8192 to 16384, as said below
- query_request: int32 [4096], P(('rep', 'blk')), parts along dimension 0, may hold values from 0 to 1
- query_offset: int32 [4096], P(('rep', 'blk')), parts along dimension 0, may hold values from 0 to 511
Outputs:
- attended: bfloat16 [4096, 4096], P(('rep', 'blk'), 'head'), parts along dimension 0
There are 4 independent parts, one for each index of `rep`. A program takes and returns all parts, laid end to end along the dimension named above; each array names one. Nothing has to cross between parts.
Inputs may be any that keep to these rules, and one draw needn't show every extreme that they name: `slot_request`: every pair of a request below 2 and a position below 16384 stands in exactly one slot. `lengths`: some request has length 16384.
All inputs are finite; a program needn't handle non-finite values.
Results may differ from a plain program's by a relative error of at most 0.0065.
Values may be sent and summed in bfloat16 or wider, within the bound.
A program may use at most 64 MiB of HBM per device.

v0:
```python
import math

import jax
import jax.numpy as jnp
from jax import lax
from jax.sharding import PartitionSpec as P

HD = 128
QH_DEV = 16


masked_score = -1e30


def lookup_length(lengths, requests):
    match = requests[:, None] == jnp.arange(lengths.shape[0], dtype=jnp.int32)[None, :]
    return jnp.sum(jnp.where(match, lengths[None, :], 0), axis=1)


def attend_block(
    state_now,
    query_rows,
    query_request,
    query_position,
    key_rows,
    value_rows,
    key_request,
    key_position,
):
    weighted, peak_old, weight_sum = state_now
    scores = jnp.einsum(
        "qgd,kd->qgk", query_rows, key_rows, preferred_element_type=jnp.float32
    ) * HD ** (-0.5)
    allowed = (query_request[:, None] == key_request[None, :]) & (
        key_position[None, :] <= query_position[:, None]
    )
    scores = jnp.where(allowed[:, None, :], scores, masked_score)
    peak_new = jnp.maximum(peak_old, jnp.max(scores, axis=2))
    raw_weight = jnp.where(allowed[:, None, :], jnp.exp(scores - peak_new[:, :, None]), 0.0)
    shrink = jnp.exp(peak_old - peak_new)
    weight_sum = weight_sum * shrink + jnp.sum(raw_weight, axis=2)
    product = jnp.einsum(
        "qgk,kd->qgd",
        raw_weight.astype(jnp.bfloat16),
        value_rows,
        preferred_element_type=jnp.float32,
    )
    weighted = weighted * shrink[:, :, None] + product
    return (weighted, peak_new, weight_sum)


def sweep_keys(
    state_now,
    query_rows,
    query_request,
    query_position,
    key_rows,
    value_rows,
    key_request,
    key_position,
):
    key_count = key_rows.shape[0]
    width = math.gcd(key_count, 4096)
    turns = key_count // width
    sliced_all = (
        key_rows.reshape(turns, width, key_rows.shape[1]),
        value_rows.reshape(turns, width, value_rows.shape[1]),
        key_request.reshape(turns, width),
        key_position.reshape(turns, width),
    )

    def one_turn(state_in, sliced):
        state_out = attend_block(
            state_in,
            query_rows,
            query_request,
            query_position,
            sliced[0],
            sliced[1],
            sliced[2],
            sliced[3],
        )
        return (state_out, None)

    state_final, unused = lax.scan(one_turn, state_now, sliced_all)
    return state_final


def shards(
    queries,
    cache_keys,
    cache_values,
    slot_request,
    slot_position,
    lengths,
    query_request,
    query_offset,
):
    row_count = queries.shape[0]
    query_position = lookup_length(lengths, query_request) - 1 - query_offset
    empty_state = (
        jnp.zeros((row_count, QH_DEV, HD), jnp.float32),
        jnp.full((row_count, QH_DEV), masked_score, jnp.float32),
        jnp.zeros((row_count, QH_DEV), jnp.float32),
    )
    query_rows = queries.reshape(row_count, QH_DEV, HD)
    weighted, peak_score, weight_sum = sweep_keys(
        empty_state,
        query_rows,
        query_request,
        query_position,
        lax.all_gather(cache_keys, "blk", axis=0, tiled=True),
        lax.all_gather(cache_values, "blk", axis=0, tiled=True),
        lax.all_gather(slot_request, "blk", axis=0, tiled=True),
        lax.all_gather(slot_position, "blk", axis=0, tiled=True),
    )
    return (weighted / weight_sum[:, :, None]).reshape(row_count, QH_DEV * HD).astype(jnp.bfloat16)


def solution(mesh):
    return jax.shard_map(
        shards,
        mesh=mesh,
        in_specs=(
            P(("rep", "blk"), "head"),
            P(("rep", "blk"), "head"),
            P(("rep", "blk"), "head"),
            P(("rep", "blk")),
            P(("rep", "blk")),
            P("rep"),
            P(("rep", "blk")),
            P(("rep", "blk")),
        ),
        out_specs=P(("rep", "blk"), "head"),
        check_vma=False,
    )
```

profile of v0, /device:TPU:16, one launch (start us, length us, event | category | flops | bytes accessed | tf_op | source)
XLA Modules:
  0.0 345.3 jit_solution(562509052610400891)
XLA Ops:
  6.5 0.7 all-gather.3.cloned.1.call-update
  7.3 0.7 all-gather.5.cloned.1.call-update
  8.0 46.3 %all_gather.12 = s32[32768]{0:T(1024)S(1)} all-gather(s32[1024]{0:T(1024)} %param.13), channel_id=1, replica_groups=mesh['blk'=32,'head'=2,'rep'=4] {'blk'}, dimensions={0}, use_global_device_ids=true | all-gather | bytes 135168 | tf_op jit(solution)/shard_map/all_gather | solution.py:114
  54.4 42.3 %all_gather.13 = s32[32768]{0:T(1024)S(1)} all-gather(s32[1024]{0:T(1024)} %param.14), channel_id=1, replica_groups=mesh['blk'=32,'head'=2,'rep'=4] {'blk'}, dimensions={0}, use_global_device_ids=true | all-gather | bytes 135168 | tf_op jit(solution)/shard_map/all_gather | solution.py:115
  96.8 0.8 fusion.21
  97.5 0.7 add_subtract_fusion
  98.2 13.4 %all-gather.3.cloned.1.call-done = bf16[32768,128]{1,0:T(8,128)(2,1)} async-done(((bf16[1024,128]{1,0:T(8,128)(2,1)}), bf16[32768,128]{1,0:T(8,128)(2,1)}) %all-gather.3.cloned.1.call-update) | async-done | bytes 8388624 | tf_op jit(solution)/shard_map/all_gather | solution.py:112
  111.6 97.9 %all-gather.5.cloned.1.call-done = bf16[32768,128]{1,0:T(8,128)(2,1)} async-done(((bf16[1024,128]{1,0:T(8,128)(2,1)}), bf16[32768,128]{1,0:T(8,128)(2,1)}) %all-gather.5.cloned.1.call-update) | async-done | bytes 8388624 | tf_op jit(solution)/shard_map/all_gather | solution.py:113
  209.6 128.0 %while.15 = (s32[]{:T(128)}, f32[32,16,128]{2,0,1:T(8,128)S(1)}, f32[32,16]{0,1:T(8,128)S(1)}, f32[32,16]{0,1:T(8,128)S(1)}, s32[32]{0:T(128)}, /*index=5*/s32[8...) while((s32[]{:T(128)}, f32[32,16,128]{2,0,1:T(8,128)S(1)}, ...), condition=%wide.region_4.5_spmd.clone, body=%wide.region_1.4_spmd.clone.sunk | while | flops 1101597184 | bytes 62129572 | solution.py:85
  209.6 0.8 compare_and_fusion.2
  210.5 5.8 %fusion.35 = (f32[32,16]{0,1:T(8,128)S(1)}, f32[4096,32,16]{0,1,2:T(8,128)}) fusion(pred[32,4096]{1,0:T(8,128)(4,1)S(1)} %compare_and_fusion.2, bf16[32,16,128]{2,0,1:T(8,128)(2,1)S(1)} %get-tuple-element.276, bf16[8,4096,128]{2,1,0:T(8,128)(2,1)} %get-tuple-element.275, s32[]{:T(128)} %get-tuple-element.254), kind=kOutput, calls=%fused_computation.2.clone.1 | convolution fusion | flops 543161856 | bytes 9701888 | tf_op jit(solution)/shard_map/while/body/eval_jaxpr/qgd,kd->qgk/dot_general | solution.py:31
  216.3 5.6 %fusion.36 = f32[32,16]{0,1:T(8,128)S(1)} fusion(f32[4096,32,16]{0,1,2:T(8,128)} %get-tuple-element.237, f32[32,16]{0,1:T(8,128)S(1)} %select_maximum_fusion.2, pred[32,4096]{1,0:T(8,128)(4,1)S(1)} %compare_and_fusion.2), kind=kLoop, calls=%fused_computation.3.clone.1 | loop fusion | flops 10485248 | bytes 8523776 | tf_op jit(solution)/shard_map/while/body/eval_jaxpr/reduce_sum | solution.py:41
  222.0 0.2 copy-done.1
  222.1 3.4 fusion.38
  225.6 0.8 compare_and_fusion.2
  226.5 5.8 %fusion.35 = (f32[32,16]{0,1:T(8,128)S(1)}, f32[4096,32,16]{0,1,2:T(8,128)}) fusion(pred[32,4096]{1,0:T(8,128)(4,1)S(1)} %compare_and_fusion.2, bf16[32,16,128]{2,0,1:T(8,128)(2,1)S(1)} %get-tuple-element.276, bf16[8,4096,128]{2,1,0:T(8,128)(2,1)} %get-tuple-element.275, s32[]{:T(128)} %get-tuple-element.254), kind=kOutput, calls=%fused_computation.2.clone.1 | convolution fusion | flops 543161856 | bytes 9701888 | tf_op jit(solution)/shard_map/while/body/eval_jaxpr/qgd,kd->qgk/dot_general | solution.py:31
  232.3 5.6 %fusion.36 = f32[32,16]{0,1:T(8,128)S(1)} fusion(f32[4096,32,16]{0,1,2:T(8,128)} %get-tuple-element.237, f32[32,16]{0,1:T(8,128)S(1)} %select_maximum_fusion.2, pred[32,4096]{1,0:T(8,128)(4,1)S(1)} %compare_and_fusion.2), kind=kLoop, calls=%fused_computation.3.clone.1 | loop fusion | flops 10485248 | bytes 8523776 | tf_op jit(solution)/shard_map/while/body/eval_jaxpr/reduce_sum | solution.py:41
  238.0 0.2 copy-done.1
  238.1 3.4 fusion.38
  241.6 0.8 compare_and_fusion.2
  242.5 5.8 %fusion.35 = (f32[32,16]{0,1:T(8,128)S(1)}, f32[4096,32,16]{0,1,2:T(8,128)}) fusion(pred[32,4096]{1,0:T(8,128)(4,1)S(1)} %compare_and_fusion.2, bf16[32,16,128]{2,0,1:T(8,128)(2,1)S(1)} %get-tuple-element.276, bf16[8,4096,128]{2,1,0:T(8,128)(2,1)} %get-tuple-element.275, s32[]{:T(128)} %get-tuple-element.254), kind=kOutput, calls=%fused_computation.2.clone.1 | convolution fusion | flops 543161856 | bytes 9701888 | tf_op jit(solution)/shard_map/while/body/eval_jaxpr/qgd,kd->qgk/dot_general | solution.py:31
  248.3 5.6 %fusion.36 = f32[32,16]{0,1:T(8,128)S(1)} fusion(f32[4096,32,16]{0,1,2:T(8,128)} %get-tuple-element.237, f32[32,16]{0,1:T(8,128)S(1)} %select_maximum_fusion.2, pred[32,4096]{1,0:T(8,128)(4,1)S(1)} %compare_and_fusion.2), kind=kLoop, calls=%fused_computation.3.clone.1 | loop fusion | flops 10485248 | bytes 8523776 | tf_op jit(solution)/shard_map/while/body/eval_jaxpr/reduce_sum | solution.py:41
  254.0 0.2 copy-done.1
  254.2 3.4 fusion.38
  257.6 0.8 compare_and_fusion.2
  258.5 5.8 %fusion.35 = (f32[32,16]{0,1:T(8,128)S(1)}, f32[4096,32,16]{0,1,2:T(8,128)}) fusion(pred[32,4096]{1,0:T(8,128)(4,1)S(1)} %compare_and_fusion.2, bf16[32,16,128]{2,0,1:T(8,128)(2,1)S(1)} %get-tuple-element.276, bf16[8,4096,128]{2,1,0:T(8,128)(2,1)} %get-tuple-element.275, s32[]{:T(128)} %get-tuple-element.254), kind=kOutput, calls=%fused_computation.2.clone.1 | convolution fusion | flops 543161856 | bytes 9701888 | tf_op jit(solution)/shard_map/while/body/eval_jaxpr/qgd,kd->qgk/dot_general | solution.py:31
  264.3 5.6 %fusion.36 = f32[32,16]{0,1:T(8,128)S(1)} fusion(f32[4096,32,16]{0,1,2:T(8,128)} %get-tuple-element.237, f32[32,16]{0,1:T(8,128)S(1)} %select_maximum_fusion.2, pred[32,4096]{1,0:T(8,128)(4,1)S(1)} %compare_and_fusion.2), kind=kLoop, calls=%fused_computation.3.clone.1 | loop fusion | flops 10485248 | bytes 8523776 | tf_op jit(solution)/shard_map/while/body/eval_jaxpr/reduce_sum | solution.py:41
  270.0 0.2 copy-done.1
  270.2 3.4 fusion.38
  273.7 0.8 compare_and_fusion.2
  274.5 5.8 %fusion.35 = (f32[32,16]{0,1:T(8,128)S(1)}, f32[4096,32,16]{0,1,2:T(8,128)}) fusion(pred[32,4096]{1,0:T(8,128)(4,1)S(1)} %compare_and_fusion.2, bf16[32,16,128]{2,0,1:T(8,128)(2,1)S(1)} %get-tuple-element.276, bf16[8,4096,128]{2,1,0:T(8,128)(2,1)} %get-tuple-element.275, s32[]{:T(128)} %get-tuple-element.254), kind=kOutput, calls=%fused_computation.2.clone.1 | convolution fusion | flops 543161856 | bytes 9701888 | tf_op jit(solution)/shard_map/while/body/eval_jaxpr/qgd,kd->qgk/dot_general | solution.py:31
  280.3 5.6 %fusion.36 = f32[32,16]{0,1:T(8,128)S(1)} fusion(f32[4096,32,16]{0,1,2:T(8,128)} %get-tuple-element.237, f32[32,16]{0,1:T(8,128)S(1)} %select_maximum_fusion.2, pred[32,4096]{1,0:T(8,128)(4,1)S(1)} %compare_and_fusion.2), kind=kLoop, calls=%fused_computation.3.clone.1 | loop fusion | flops 10485248 | bytes 8523776 | tf_op jit(solution)/shard_map/while/body/eval_jaxpr/reduce_sum | solution.py:41
  286.0 0.2 copy-done.1
  286.2 3.4 fusion.38
  289.7 0.8 compare_and_fusion.2
  290.5 5.8 %fusion.35 = (f32[32,16]{0,1:T(8,128)S(1)}, f32[4096,32,16]{0,1,2:T(8,128)}) fusion(pred[32,4096]{1,0:T(8,128)(4,1)S(1)} %compare_and_fusion.2, bf16[32,16,128]{2,0,1:T(8,128)(2,1)S(1)} %get-tuple-element.276, bf16[8,4096,128]{2,1,0:T(8,128)(2,1)} %get-tuple-element.275, s32[]{:T(128)} %get-tuple-element.254), kind=kOutput, calls=%fused_computation.2.clone.1 | convolution fusion | flops 543161856 | bytes 9701888 | tf_op jit(solution)/shard_map/while/body/eval_jaxpr/qgd,kd->qgk/dot_general | solution.py:31
  296.4 5.6 %fusion.36 = f32[32,16]{0,1:T(8,128)S(1)} fusion(f32[4096,32,16]{0,1,2:T(8,128)} %get-tuple-element.237, f32[32,16]{0,1:T(8,128)S(1)} %select_maximum_fusion.2, pred[32,4096]{1,0:T(8,128)(4,1)S(1)} %compare_and_fusion.2), kind=kLoop, calls=%fused_computation.3.clone.1 | loop fusion | flops 10485248 | bytes 8523776 | tf_op jit(solution)/shard_map/while/body/eval_jaxpr/reduce_sum | solution.py:41
  302.0 0.2 copy-done.1
  302.2 3.4 fusion.38
  305.7 0.8 compare_and_fusion.2
  306.5 5.8 %fusion.35 = (f32[32,16]{0,1:T(8,128)S(1)}, f32[4096,32,16]{0,1,2:T(8,128)}) fusion(pred[32,4096]{1,0:T(8,128)(4,1)S(1)} %compare_and_fusion.2, bf16[32,16,128]{2,0,1:T(8,128)(2,1)S(1)} %get-tuple-element.276, bf16[8,4096,128]{2,1,0:T(8,128)(2,1)} %get-tuple-element.275, s32[]{:T(128)} %get-tuple-element.254), kind=kOutput, calls=%fused_computation.2.clone.1 | convolution fusion | flops 543161856 | bytes 9701888 | tf_op jit(solution)/shard_map/while/body/eval_jaxpr/qgd,kd->qgk/dot_general | solution.py:31
  312.4 5.6 %fusion.36 = f32[32,16]{0,1:T(8,128)S(1)} fusion(f32[4096,32,16]{0,1,2:T(8,128)} %get-tuple-element.237, f32[32,16]{0,1:T(8,128)S(1)} %select_maximum_fusion.2, pred[32,4096]{1,0:T(8,128)(4,1)S(1)} %compare_and_fusion.2), kind=kLoop, calls=%fused_computation.3.clone.1 | loop fusion | flops 10485248 | bytes 8523776 | tf_op jit(solution)/shard_map/while/body/eval_jaxpr/reduce_sum | solution.py:41
  318.2 3.4 fusion.38
  321.7 0.8 compare_and_fusion.2
  322.5 5.8 %fusion.35 = (f32[32,16]{0,1:T(8,128)S(1)}, f32[4096,32,16]{0,1,2:T(8,128)}) fusion(pred[32,4096]{1,0:T(8,128)(4,1)S(1)} %compare_and_fusion.2, bf16[32,16,128]{2,0,1:T(8,128)(2,1)S(1)} %get-tuple-element.276, bf16[8,4096,128]{2,1,0:T(8,128)(2,1)} %get-tuple-element.275, s32[]{:T(128)} %get-tuple-element.254), kind=kOutput, calls=%fused_computation.2.clone.1 | convolution fusion | flops 543161856 | bytes 9701888 | tf_op jit(solution)/shard_map/while/body/eval_jaxpr/qgd,kd->qgk/dot_general | solution.py:31
  328.4 5.6 %fusion.36 = f32[32,16]{0,1:T(8,128)S(1)} fusion(f32[4096,32,16]{0,1,2:T(8,128)} %get-tuple-element.237, f32[32,16]{0,1:T(8,128)S(1)} %select_maximum_fusion.2, pred[32,4096]{1,0:T(8,128)(4,1)S(1)} %compare_and_fusion.2), kind=kLoop, calls=%fused_computation.3.clone.1 | loop fusion | flops 10485248 | bytes 8523776 | tf_op jit(solution)/shard_map/while/body/eval_jaxpr/reduce_sum | solution.py:41
  334.2 3.4 fusion.38
  337.6 0.8 copy_bitcast_fusion
  (52 shorter events, 0.8 us)
Async XLA Ops:
  6.5 91.7 %copy-start = (bf16[32,2048]{1,0:T(8,128)(2,1)S(1)}, bf16[32,2048]{1,0:T(8,128)(2,1)}, u32[]{:S(2)}) copy-start(bf16[32,2048]{1,0:T(8,128)(2,1)} %param.10) | copy-start | bytes 393220
  6.5 105.1 %all-gather.3.cloned.1.call-start = ((), (), s32[]{:S(2)}) async-start(), calls=%async_computation | async-start | bytes 8650752 | tf_op jit(solution)/shard_map/all_gather | solution.py:112
  7.3 202.3 %all-gather.5.cloned.1.call-start = ((), (), s32[]{:S(2)}) async-start(), calls=%async_computation.1 | async-start | bytes 8650752 | tf_op jit(solution)/shard_map/all_gather | solution.py:113
  216.3 5.8 %copy-start.1 = (f32[4096,32,16]{0,1,2:T(8,128)S(1)}, f32[4096,32,16]{0,1,2:T(8,128)}, u32[]{:S(2)}) copy-start(f32[4096,32,16]{0,1,2:T(8,128)} %get-tuple-element.237) | copy-start | bytes 25165828 | tf_op jit(solution)/shard_map/while
  232.3 5.8 %copy-start.1 = (f32[4096,32,16]{0,1,2:T(8,128)S(1)}, f32[4096,32,16]{0,1,2:T(8,128)}, u32[]{:S(2)}) copy-start(f32[4096,32,16]{0,1,2:T(8,128)} %get-tuple-element.237) | copy-start | bytes 25165828 | tf_op jit(solution)/shard_map/while
  248.3 5.8 %copy-start.1 = (f32[4096,32,16]{0,1,2:T(8,128)S(1)}, f32[4096,32,16]{0,1,2:T(8,128)}, u32[]{:S(2)}) copy-start(f32[4096,32,16]{0,1,2:T(8,128)} %get-tuple-element.237) | copy-start | bytes 25165828 | tf_op jit(solution)/shard_map/while
  264.3 5.8 %copy-start.1 = (f32[4096,32,16]{0,1,2:T(8,128)S(1)}, f32[4096,32,16]{0,1,2:T(8,128)}, u32[]{:S(2)}) copy-start(f32[4096,32,16]{0,1,2:T(8,128)} %get-tuple-element.237) | copy-start | bytes 25165828 | tf_op jit(solution)/shard_map/while
  280.3 5.8 %copy-start.1 = (f32[4096,32,16]{0,1,2:T(8,128)S(1)}, f32[4096,32,16]{0,1,2:T(8,128)}, u32[]{:S(2)}) copy-start(f32[4096,32,16]{0,1,2:T(8,128)} %get-tuple-element.237) | copy-start | bytes 25165828 | tf_op jit(solution)/shard_map/while
  296.3 5.8 %copy-start.1 = (f32[4096,32,16]{0,1,2:T(8,128)S(1)}, f32[4096,32,16]{0,1,2:T(8,128)}, u32[]{:S(2)}) copy-start(f32[4096,32,16]{0,1,2:T(8,128)} %get-tuple-element.237) | copy-start | bytes 25165828 | tf_op jit(solution)/shard_map/while
  312.4 5.8 %copy-start.1 = (f32[4096,32,16]{0,1,2:T(8,128)S(1)}, f32[4096,32,16]{0,1,2:T(8,128)}, u32[]{:S(2)}) copy-start(f32[4096,32,16]{0,1,2:T(8,128)} %get-tuple-element.237) | copy-start | bytes 25165828 | tf_op jit(solution)/shard_map/while
  328.4 5.8 %copy-start.1 = (f32[4096,32,16]{0,1,2:T(8,128)S(1)}, f32[4096,32,16]{0,1,2:T(8,128)}, u32[]{:S(2)}) copy-start(f32[4096,32,16]{0,1,2:T(8,128)} %get-tuple-element.237) | copy-start | bytes 25165828 | tf_op jit(solution)/shard_map/while
Sparse Core Ops, SparseCore 0:
  9.9 101.6 all-gather.2
  114.2 95.3 all-gather.4
where the time goes:
time: 347 us; the launch traced here: 345 us
  waiting for transfers between devices  113 us (33%)
  blocking collectives  88.7 us (26%)
  matrix products  74.2 us (21%)
  other arithmetic  54.1 us (16%)
  between operations  13.4 us (4%)
    all_gather x1, waiting for transfers between devices, shards(): lax.all_gather(cache_values, 'blk', axis=0, tiled=True)  97.9 us
    dot_general x8, matrix products, attend_block(): jnp.einsum('qgd,kd->qgk', query_rows, key_rows, preferred_element_type=jn...  46.8 us
    all_gather x1, blocking collectives, shards(): lax.all_gather(slot_request, 'blk', axis=0, tiled=True)  46.3 us
    reduce_sum x8, other arithmetic, attend_block(): weight_sum = weight_sum * shrink + jnp.sum(raw_weight, axis=2)  45.2 us
    all_gather x1, blocking collectives, shards(): lax.all_gather(slot_position, 'blk', axis=0, tiled=True)  42.3 us
    dot_general x8, matrix products, attend_block(): jnp.einsum('qgk,kd->qgd', raw_weight.astype(jnp.bfloat16), value_rows, pr...  27.4 us
    all_gather x1, waiting for transfers between devices, shards(): lax.all_gather(cache_keys, 'blk', axis=0, tiled=True)  13.4 us
  transfers between devices with their start and end apart: 2, of which 2 were waited for; matrix products, arithmetic and copies ran while one was open for 0% of the time, Pallas kernels for 0%

commit v1 on v0

v1 whole, which is shorter than its diff:
```python
import functools

import jax
import jax.numpy as jnp
from jax import lax
from jax.experimental import pallas as pl
from jax.experimental.pallas import tpu as pltpu
from jax.sharding import PartitionSpec as P

HD = 128
QH_DEV = 16
TOK = 32
ROWS = TOK * QH_DEV
SLOT = 1024
HALF = SLOT // 2
QW = QH_DEV * HD
NZ = 8
NX = 4
SCALE = 1.4426950408889634 * HD ** -0.5
MASKED = -1e30
FLOOR = -1e29
REQ_STEP = 65536.0
SOFT_ROWS = 128
MESH = pl.DeviceIdType.MESH
F32 = jnp.float32
BF16 = jnp.bfloat16

PAIRS = (
    (0, 0), (1, 0), (7, 0), (0, 1), (1, 1), (7, 1), (2, 0), (6, 0),
    (2, 1), (6, 1), (3, 0), (5, 0), (3, 1), (5, 1), (4, 0), (4, 1),
    (4, 2), (4, 3), (3, 2), (3, 3), (5, 2), (5, 3), (2, 2), (2, 3),
    (6, 2), (6, 3), (1, 2), (1, 3), (7, 2), (7, 3), (0, 2), (0, 3),
)
N = len(PAIRS)


def first_use(kind, value):
    return min(i for i, pair in enumerate(PAIRS) if pair[kind] == value)


def last_use(query):
    return max(i for i, pair in enumerate(PAIRS) if pair[0] == query)


def pick(index, column):
    value = jnp.int32(PAIRS[N - 1][column])
    for i in range(N - 2, -1, -1):
        value = jnp.where(index <= i, jnp.int32(PAIRS[i][column]), value)
    return value


def kernel(
    len_ref, qreq_ref, qoff_ref, sreq_ref, spos_ref, q_hbm, k_hbm, v_hbm,
    out_ref,
    qs, ks, vs, code, s0, s1, p0, p1, a0, a1, acc, peak,
    sent, sent_stat, got, got_stat,
    local_sem, kv_send, kv_recv, q_send, q_recv, part_send, part_recv,
):
    me = lax.axis_index("blk")
    z = me // NX
    x = lax.rem(me, NX)
    right = z * NX + lax.rem(x + 1, NX)
    left = z * NX + lax.rem(x + NX - 1, NX)
    up = lax.rem(z + 1, NZ) * NX + x
    down = lax.rem(z + NZ - 1, NZ) * NX + x

    barrier = pltpu.get_barrier_semaphore()
    for other in (up, down, right, left):
        pl.semaphore_signal(barrier, inc=1, device_id={"blk": other}, device_id_type=MESH)

    own = [
        pltpu.make_async_copy(q_hbm, qs.at[0, :, pl.ds(0, QW)], local_sem.at[0]),
        pltpu.make_async_copy(k_hbm, ks.at[0], local_sem.at[1]),
        pltpu.make_async_copy(v_hbm, vs.at[0, :, pl.ds(0, HD)], local_sem.at[2]),
    ]
    for copy in own:
        copy.start()

    request = qreq_ref[...]
    length = jnp.where(request == 0, len_ref[0], len_ref[1])
    position = length - 1 - qoff_ref[...]
    eye = lax.broadcasted_iota(jnp.int32, (TOK, TOK), 0) == lax.broadcasted_iota(jnp.int32, (TOK, TOK), 1)

    def column(row):
        return jnp.sum(jnp.where(eye, jnp.broadcast_to(row, (TOK, TOK)), 0), axis=1, keepdims=True)

    lane = lax.broadcasted_iota(jnp.int32, (TOK, HD), 1)
    position = column(position)
    meta = jnp.where(
        lane == 0, column(request),
        jnp.where(lane == 1, position // 128, jnp.where(lane == 2, position % 128, 0)),
    )
    qs[0, :, QW:] = meta.astype(F32).astype(BF16)
    code[0] = sreq_ref[...].astype(F32) * REQ_STEP + spos_ref[...].astype(F32)
    vs[:, :, HD:] = jnp.ones((NX, SLOT, HD), BF16)
    acc[...] = jnp.zeros_like(acc)
    peak[...] = jnp.full(peak.shape, FLOOR, F32)
    p1[...] = jnp.zeros_like(p1)
    a1[...] = jnp.ones_like(a1)
    for copy in own:
        copy.wait()
    pl.semaphore_wait(barrier, 4)

    def remote(src, dst, send_sem, recv_sem, other):
        return pltpu.make_async_remote_copy(
            src_ref=src, dst_ref=dst, send_sem=send_sem, recv_sem=recv_sem,
            device_id={"blk": other}, device_id_type=MESH,
        )

    def kv_copies(chunk, src_slot, src_at, dst_slot, dst_at, other):
        src = pl.ds(src_at, HALF)
        dst = pl.ds(dst_at, HALF)
        return [
            remote(ks.at[src_slot, src], ks.at[dst_slot, dst],
                   kv_send.at[chunk, 0], kv_recv.at[chunk, 0], other),
            remote(vs.at[src_slot, src, pl.ds(0, HD)], vs.at[dst_slot, dst, pl.ds(0, HD)],
                   kv_send.at[chunk, 1], kv_recv.at[chunk, 1], other),
            remote(code.at[src_slot, :, src], code.at[dst_slot, :, dst],
                   kv_send.at[chunk, 2], kv_recv.at[chunk, 2], other),
        ]

    kv = [
        kv_copies(0, 0, HALF, 1, 0, right),
        kv_copies(1, 0, 0, 1, HALF, left),
        kv_copies(2, 0, 0, 2, 0, right),
        kv_copies(3, 0, HALF, 2, HALF, left),
        kv_copies(4, 1, 0, 3, HALF, right),
        kv_copies(5, 1, HALF, 3, 0, left),
    ]
    qc = {
        7: remote(qs.at[0], qs.at[7], q_send.at[7], q_recv.at[7], up),
        6: remote(qs.at[7], qs.at[6], q_send.at[6], q_recv.at[6], up),
        5: remote(qs.at[6], qs.at[5], q_send.at[5], q_recv.at[5], up),
        4: remote(qs.at[5, pl.ds(0, TOK // 2)], qs.at[4, pl.ds(0, TOK // 2)],
                  q_send.at[4], q_recv.at[4], up),
        1: remote(qs.at[0], qs.at[1], q_send.at[1], q_recv.at[1], down),
        2: remote(qs.at[1], qs.at[2], q_send.at[2], q_recv.at[2], down),
        3: remote(qs.at[2], qs.at[3], q_send.at[3], q_recv.at[3], down),
        0: remote(qs.at[3, pl.ds(TOK // 2, TOK // 2)], qs.at[4, pl.ds(TOK // 2, TOK // 2)],
                  q_send.at[0], q_recv.at[0], down),
    }
    def part_copies(src_slot, dst_slot, begin, count, other):
        rows = pl.ds(begin, count)
        stats = pl.ds(begin // HD, count // HD)
        return [
            remote(sent.at[src_slot, rows], got.at[dst_slot, rows],
                   part_send.at[dst_slot, 0], part_recv.at[dst_slot, 0], other),
            remote(sent_stat.at[src_slot, stats], got_stat.at[dst_slot, stats],
                   part_send.at[dst_slot, 1], part_recv.at[dst_slot, 1], other),
        ]

    part = {
        3: part_copies(4, 3, 0, ROWS // 2, up),
        2: part_copies(3, 2, 0, ROWS, up),
        1: part_copies(2, 1, 0, ROWS, up),
        0: part_copies(1, 0, 0, ROWS, up),
        5: part_copies(4, 5, ROWS // 2, ROWS // 2, down),
        6: part_copies(5, 6, 0, ROWS, down),
        7: part_copies(6, 7, 0, ROWS, down),
        4: part_copies(7, 4, 0, ROWS, down),
    }

    def start(copies):
        for copy in copies:
            copy.start()

    start([qc[7], qc[1]])
    for chunk in range(4):
        start(kv[chunk])

    eye_hd = lax.broadcasted_iota(jnp.int32, (HD, HD), 0) == lax.broadcasted_iota(jnp.int32, (HD, HD), 1)

    def to_row(block):
        return jnp.sum(jnp.where(eye_hd, block, 0.0), axis=0, keepdims=True)

    def to_column(row):
        return jnp.sum(jnp.where(eye_hd, jnp.broadcast_to(row, (HD, HD)), 0.0), axis=1, keepdims=True)

    def state(query, g):
        rows = pl.ds(g * HD, HD)
        return peak[query, rows, :], acc[query, rows, 0:HD], acc[query, rows, HD:]

    def merge(mine, slot, g):
        rows = pl.ds(g * HD, HD)
        m, w, l = mine
        m_in = to_column(got_stat[slot, g, 0:1, :])
        l_in = to_column(got_stat[slot, g, 1:2, :])
        m_new = jnp.maximum(m, m_in)
        keep = jnp.exp2(m - m_new)
        take = jnp.exp2(m_in - m_new)
        return m_new, w * keep + got[slot, rows, :].astype(F32) * take, l * keep + l_in * take

    def finish(query):
        if query == 3:
            merged = (0, 1)
        elif query == 5:
            merged = (2, 3)
        elif query == 4:
            merged = ()
        else:
            merged = (0, 1, 2, 3)
        if merged:
            for copy in part[query]:
                copy.wait_recv()
        for g in range(4):
            now = state(query, g)
            if g in merged:
                now = merge(now, query, g)
            m, w, l = now
            sent[query, pl.ds(g * HD, HD), :] = w.astype(BF16)
            sent_stat[query, g, 0:1, :] = to_row(m)
            sent_stat[query, g, 1:2, :] = to_row(l)
        if query == 4:
            start(part[3])
            start(part[5])
        elif query < 4:
            start(part[query - 1])
        else:
            start(part[(query + 1) if query < 7 else 4])

    actions = {}

    def at(stage, action):
        actions.setdefault(stage, []).append(action)

    def take_query(low, high, forward):
        def action():
            for copy in low:
                copy.wait_recv()
            for copy in high:
                copy.wait_recv()
            start(forward)
        return action

    def take_keys(chunks):
        def action():
            for chunk in chunks:
                for copy in kv[chunk]:
                    copy.wait_recv()
        return action

    def forward_keys():
        start(kv[4])
        start(kv[5])

    at(first_use(0, 1) - 1, take_query([qc[1]], [qc[7]], [qc[2], qc[6]]))
    at(first_use(0, 2) - 1, take_query([qc[2]], [qc[6]], [qc[3], qc[5]]))
    at(first_use(0, 3) - 1, take_query([qc[3]], [qc[5]], [qc[0], qc[4]]))
    at(first_use(0, 4) - 1, take_query([qc[0]], [qc[4]], []))
    at(first_use(1, 1) - 1, take_keys((0, 1)))
    at(first_use(1, 1) - 1 + FORWARD_AFTER, forward_keys)
    at(first_use(1, 2) - 1, take_keys((2, 3)))
    at(first_use(1, 3) - 1, take_keys((4, 5)))
    for query in (4, 3, 5, 2, 6, 1, 7):
        at(last_use(query) + 2, functools.partial(finish, query))

    def do(stage_index, parity):
        for stage in sorted(actions):
            if stage % 2 == parity and stage < N:
                @pl.when(stage_index == stage)
                def _():
                    for action in actions[stage]:
                        action()

    def scores(query, key, into):
        q = jnp.concatenate([qs[query, :, pl.ds(h * HD, HD)] for h in range(QH_DEV)], axis=0)
        into[...] = lax.dot_general(q, ks[key], (((1,), (1,)), ((), ())), preferred_element_type=F32)

    def softmax(query, key, scored, weights, shrink):
        meta = qs[query, :, QW:].astype(F32)
        low = meta[:, 0:1] * REQ_STEP
        high = low + (meta[:, 1:2] * 128.0 + meta[:, 2:3])
        where = code[key]
        bias = jnp.where((where >= low) & (where <= high), 0.0, MASKED)
        for r in range(ROWS // SOFT_ROWS):
            rows = pl.ds(r * SOFT_ROWS, SOFT_ROWS)
            heads = SOFT_ROWS // TOK
            s = (scored[rows, :].reshape(heads, TOK, SLOT) * SCALE + bias[None]).reshape(SOFT_ROWS, SLOT)
            m_old = peak[query, rows, :]
            m_new = jnp.maximum(m_old, jnp.max(s, axis=1, keepdims=True))
            shrink[rows, :] = jnp.exp2(m_old - m_new)
            weights[rows, :] = jnp.exp2(s - m_new[:, 0:1]).astype(BF16)
            peak[query, rows, :] = m_new

    def values(query, key, weights, shrink):
        o = jnp.dot(weights[...], vs[key], preferred_element_type=F32)
        keep = shrink[...]
        acc[query, :, 0:HD] = acc[query, :, 0:HD] * keep + o[:, 0:HD]
        acc[query, :, HD:] = acc[query, :, HD:] * keep + o[:, HD:]

    scores(0, 0, s0)

    def body(j, carry):
        before, now = carry
        i = 2 * j
        do(i, 0)
        after = (pick(i + 1, 0), pick(i + 1, 1))
        scores(*after, s1)
        softmax(*now, s0, p0, a0)
        values(*before, p1, a1)
        do(i + 1, 1)
        last = (pick(i + 2, 0), pick(i + 2, 1))
        scores(*last, s0)
        softmax(*after, s1, p1, a1)
        values(*now, p0, a0)
        return after, last

    zero = jnp.int32(0)
    first = (zero, zero)
    lax.fori_loop(0, N // 2, body, (first, first))
    values(*PAIRS[N - 1], p1, a1)
    for stage in sorted(actions):
        if stage >= N:
            for action in actions[stage]:
                action()

    for slot in (0, 4):
        for copy in part[slot]:
            copy.wait_recv()
    for g in range(4):
        now = merge(merge(state(0, g), 0, g), 4, g)
        o = (now[1] / now[2]).astype(BF16)
        for h in range(4):
            out_ref[:, pl.ds((g * 4 + h) * HD, HD)] = o[h * TOK:(h + 1) * TOK, :]

    for copies in kv:
        for copy in copies:
            copy.wait_send()
    for copy in qc.values():
        copy.wait_send()
    for copies in part.values():
        for copy in copies:
            copy.wait_send()


FORWARD_AFTER = 4


def shards(
    queries,
    cache_keys,
    cache_values,
    slot_request,
    slot_position,
    lengths,
    query_request,
    query_offset,
):
    vmem = pl.BlockSpec(memory_space=pltpu.VMEM)
    hbm = pl.BlockSpec(memory_space=pl.ANY)
    dma = pltpu.SemaphoreType.DMA
    return pl.pallas_call(
        kernel,
        out_shape=jax.ShapeDtypeStruct((TOK, QW), BF16),
        in_specs=[pl.BlockSpec(memory_space=pltpu.SMEM), vmem, vmem, vmem, vmem, hbm, hbm, hbm],
        out_specs=vmem,
        scratch_shapes=[
            pltpu.VMEM((NZ, TOK, QW + HD), BF16),
            pltpu.VMEM((NX, SLOT, HD), BF16),
            pltpu.VMEM((NX, SLOT, 2 * HD), BF16),
            pltpu.VMEM((NX, 1, SLOT), F32),
            pltpu.VMEM((ROWS, SLOT), F32),
            pltpu.VMEM((ROWS, SLOT), F32),
            pltpu.VMEM((ROWS, SLOT), BF16),
            pltpu.VMEM((ROWS, SLOT), BF16),
            pltpu.VMEM((ROWS, HD), F32),
            pltpu.VMEM((ROWS, HD), F32),
            pltpu.VMEM((NZ, ROWS, 2 * HD), F32),
            pltpu.VMEM((NZ, ROWS, HD), F32),
            pltpu.VMEM((NZ, ROWS, HD), BF16),
            pltpu.VMEM((NZ, 4, 8, HD), F32),
            pltpu.VMEM((NZ, ROWS, HD), BF16),
            pltpu.VMEM((NZ, 4, 8, HD), F32),
            dma((3,)),
            dma((6, 3)),
            dma((6, 3)),
            dma((NZ,)),
            dma((NZ,)),
            dma((NZ, 2)),
            dma((NZ, 2)),
        ],
        compiler_params=pltpu.CompilerParams(
            collective_id=0, has_side_effects=True, vmem_limit_bytes=48 * 2 ** 20
        ),
        cost_estimate=pl.CostEstimate(
            flops=4 * ROWS * SLOT * HD * N, bytes_accessed=2 ** 20, transcendentals=ROWS * SLOT * N
        ),
        name="ring_attention",
    )(
        lengths,
        query_request.reshape(1, TOK),
        query_offset.reshape(1, TOK),
        slot_request.reshape(1, SLOT),
        slot_position.reshape(1, SLOT),
        queries,
        cache_keys,
        cache_values,
    )


def solution(mesh):
    return jax.shard_map(
        shards,
        mesh=mesh,
        in_specs=(
            P(("rep", "blk"), "head"),
            P(("rep", "blk"), "head"),
            P(("rep", "blk"), "head"),
            P(("rep", "blk")),
            P(("rep", "blk")),
            P("rep"),
            P(("rep", "blk")),
            P(("rep", "blk")),
        ),
        out_specs=P(("rep", "blk"), "head"),
        check_vma=False,
    )
```

time: 347 us -> 63.7 us (0.18)
  waiting for transfers between devices: 113 us -> 0 us
  blocking collectives: 88.7 us -> 0 us
  matrix products: 74.2 us -> 0 us
  Pallas kernels: 0 us -> 58.6 us
  other arithmetic: 54.1 us -> 0 us
  between operations: 13.4 us -> 0.03 us
    all_gather x2 -> x0, waiting for transfers between devices: 111 us -> none  [the longest x1 97.9 us: shards(): lax.all_gather(cache_values, 'blk', axis=0, tiled=True)]
    all_gather x2 -> x0, blocking collectives: 88.7 us -> none  [the longest x1 46.3 us: shards(): lax.all_gather(slot_request, 'blk', axis=0, tiled=True)]
    dot_general x16 -> x0, matrix products: 74.2 us -> none  [the longest x8 46.8 us: attend_block(): jnp.einsum('qgd,kd->qgk', query_rows, key_rows, preferred_element_type=jn...]
    pallas_call x0 -> x1, Pallas kernels: none -> 58.6 us  [shards(): pl.pallas_call(kernel, out_shape=jax.ShapeDtypeStruct((TOK, QW), BF16), i...]
    reduce_sum x9 -> x0, other arithmetic: 45.9 us -> none  [the longest x8 45.2 us: attend_block(): weight_sum = weight_sum * shrink + jnp.sum(raw_weight, axis=2)]
    and x8 -> x0, other arithmetic: 6.62 us -> none  [attend_block(): (query_request[:, None] == key_request[None, :]) & (key_position[None, :]...]
    unnamed x3 -> x17, local copies, waits for them, and re-layouts: 0.03 us -> 4.84 us
  transfers between devices with their start and end apart: 2 -> 0, of which waited for: 2 -> 0; matrix products, arithmetic and copies ran while one was open for 0% -> 0% of each run, Pallas kernels for 0% -> 0%
where the time goes in v1:
time: 63.7 us; the launch traced here: 63.5 us
  Pallas kernels  58.6 us (92%)
  local copies, waits for them, and re-layouts  4.84 us (8%)
    pallas_call x1, Pallas kernels, shards(): pl.pallas_call(kernel, out_shape=jax.ShapeDtypeStruct((TOK, QW), BF16), i...  58.6 us
    unnamed x17, local copies, waits for them, and re-layouts  4.84 us

profile of v1, /device:TPU:16, one launch (start us, length us, event | category | flops | bytes accessed | tf_op | source)
XLA Modules:
  0.0 63.5 jit_solution(2687584750736440070)
XLA Ops:
  0.0 0.0 copy-start.3
  0.0 0.0 copy-start.5
  0.0 0.0 copy-start.6
  0.0 0.0 copy-start.7
  0.0 0.7 %copy-done.3 = s32[1024]{0:T(1024)S(1)} copy-done((s32[1024]{0:T(1024)S(1)}, s32[1024]{0:T(1024)}, u32[]{:S(2)}) %copy-start.3) | copy-done | bytes 4120
  0.7 0.0 copy-done.5
  0.7 0.0 copy-done.6
  0.7 0.0 copy-done.7
  0.7 0.0 copy-start
  0.7 0.9 %copy-done = bf16[1024,128]{1,0:T(8,128)(2,1)S(1)} copy-done((bf16[1024,128]{1,0:T(8,128)(2,1)S(1)}, bf16[1024,128]{1,0:T(8,128)(2,1)}, u32[]{:S(2)}) %copy-start) | copy-done | bytes 262168
  1.7 0.0 copy-start.1
  1.7 0.9 %copy-done.1 = bf16[1024,128]{1,0:T(8,128)(2,1)S(1)} copy-done((bf16[1024,128]{1,0:T(8,128)(2,1)S(1)}, bf16[1024,128]{1,0:T(8,128)(2,1)}, u32[]{:S(2)}) %copy-start.1) | copy-done | bytes 262168
  2.6 0.0 copy-start.2
  2.6 0.9 %copy-done.2 = bf16[32,2048]{1,0:T(8,128)(2,1)S(1)} copy-done((bf16[32,2048]{1,0:T(8,128)(2,1)S(1)}, bf16[32,2048]{1,0:T(8,128)(2,1)}, u32[]{:S(2)}) %copy-start.2) | copy-done | bytes 131096
  3.5 0.0 copy-start.4
  3.5 0.7 %copy-done.4 = s32[1024]{0:T(1024)S(1)} copy-done((s32[1024]{0:T(1024)S(1)}, s32[1024]{0:T(1024)}, u32[]{:S(2)}) %copy-start.4) | copy-done | bytes 4120
  4.2 58.6 %ring_attention.1 = bf16[32,2048]{1,0:T(8,128)(2,1)S(1)} custom-call(s32[2]{0:T(128)S(1)} %copy-done.5, s32[1,32]{1,0:T(1,128)S(1)} %bitcast.6, s32[1,32]{1,0:T(1,128)S(1)} %bitcast.7, s32[1,1024]{1,0:T(1,128)S(1)} %bitcast.4, s32[1,1024]{1,0:T(1,128)S(1)} %bitcast.5, bf16[32,2048]{1,0:T(8,128)(2,1)S(1)} %copy-done.2, bf16[1024,128]{1,0:T(8,128)(2,1)S(1)} %copy-done, ...), custom_call_target="tpu_custom_call" | custom-call | flops 8589934592 | bytes 1048576 | tf_op jit(solution)/shard_map/ring_attention/pallas_call | solution.py:352
  62.8 0.7 %copy.10 = bf16[32,2048]{1,0:T(8,128)(2,1)} copy(bf16[32,2048]{1,0:T(8,128)(2,1)S(1)} %ring_attention.1) | data formatting | bytes 262144
Async XLA Ops:
  0.0 0.7 %copy-start.3 = (s32[1024]{0:T(1024)S(1)}, s32[1024]{0:T(1024)}, u32[]{:S(2)}) copy-start(s32[1024]{0:T(1024)} %param.11) | copy-start | bytes 12292
  0.0 0.7 %copy-start.5 = (s32[2]{0:T(128)S(1)}, s32[2]{0:T(128)}, u32[]{:S(2)}) copy-start(s32[2]{0:T(128)} %len_ref.1) | copy-start | bytes 28
  0.0 0.7 %copy-start.6 = (s32[32]{0:T(128)S(1)}, s32[32]{0:T(128)}, u32[]{:S(2)}) copy-start(s32[32]{0:T(128)} %param.14) | copy-start | bytes 388
  0.0 0.7 %copy-start.7 = (s32[32]{0:T(128)S(1)}, s32[32]{0:T(128)}, u32[]{:S(2)}) copy-start(s32[32]{0:T(128)} %param.15) | copy-start | bytes 388
  0.7 0.9 %copy-start = (bf16[1024,128]{1,0:T(8,128)(2,1)S(1)}, bf16[1024,128]{1,0:T(8,128)(2,1)}, u32[]{:S(2)}) copy-start(bf16[1024,128]{1,0:T(8,128)(2,1)} %k_hbm.1) | copy-start | bytes 786436
  1.7 0.9 %copy-start.1 = (bf16[1024,128]{1,0:T(8,128)(2,1)S(1)}, bf16[1024,128]{1,0:T(8,128)(2,1)}, u32[]{:S(2)}) copy-start(bf16[1024,128]{1,0:T(8,128)(2,1)} %v_hbm.1) | copy-start | bytes 786436
  2.6 0.9 %copy-start.2 = (bf16[32,2048]{1,0:T(8,128)(2,1)S(1)}, bf16[32,2048]{1,0:T(8,128)(2,1)}, u32[]{:S(2)}) copy-start(bf16[32,2048]{1,0:T(8,128)(2,1)} %q_hbm.1) | copy-start | bytes 393220
  3.5 0.7 %copy-start.4 = (s32[1024]{0:T(1024)S(1)}, s32[1024]{0:T(1024)}, u32[]{:S(2)}) copy-start(s32[1024]{0:T(1024)} %param.12) | copy-start | bytes 12292

commit v2 on v1

v2 whole, which is shorter than its diff:
```python
import functools

import jax
import jax.numpy as jnp
from jax import lax
from jax.experimental import pallas as pl
from jax.experimental.pallas import tpu as pltpu
from jax.sharding import PartitionSpec as P

HD = 128
QH_DEV = 16
TOK = 32
ROWS = TOK * QH_DEV
SLOT = 1024
HALF = SLOT // 2
QW = QH_DEV * HD
NZ = 8
NX = 4
SCALE = 1.4426950408889634 * HD ** -0.5
MASKED = -1e30
FLOOR = -1e29
REQ_STEP = 65536.0
SOFT_ROWS = 128
MESH = pl.DeviceIdType.MESH
F32 = jnp.float32
BF16 = jnp.bfloat16

PAIRS = (
    (0, 0), (1, 0), (7, 0), (0, 1), (1, 1), (7, 1), (4, 0), (4, 1),
    (4, 2), (1, 2), (7, 2), (3, 0), (5, 0), (3, 1), (5, 1), (3, 2),
    (5, 2), (2, 0), (3, 3), (5, 3), (4, 3), (1, 3), (7, 3), (2, 1),
    (2, 2), (2, 3), (6, 0), (6, 1), (6, 2), (6, 3), (0, 2), (0, 3),
)
N = len(PAIRS)


def first_use(kind, value):
    return min(i for i, pair in enumerate(PAIRS) if pair[kind] == value)


def last_use(query):
    return max(i for i, pair in enumerate(PAIRS) if pair[0] == query)


def kernel(
    len_hbm, qreq_hbm, qoff_hbm, sreq_hbm, spos_hbm, q_hbm, k_hbm, v_hbm,
    out_ref,
    len_ref, qreq_ref, qoff_ref, sreq_ref, spos_ref,
    qs, ks, vs, code, b0, b1, s0, s1, p0, p1, a0, a1, acc, peak,
    sent, sent_stat, got, got_stat,
    local_sem, kv_send, kv_recv, q_send, q_recv, part_send, part_recv,
):
    me = lax.axis_index("blk")
    z = me // NX
    x = lax.rem(me, NX)

    def along_z(step):
        return lax.rem(z + step + NZ, NZ) * NX + x

    right = z * NX + lax.rem(x + 1, NX)
    left = z * NX + lax.rem(x + NX - 1, NX)
    up, up2, far, down2, down = (along_z(step) for step in (1, 2, 4, -2, -1))

    barrier = pltpu.get_barrier_semaphore()
    for other in (up, down, right, left, up2, down2, far):
        pl.semaphore_signal(barrier, inc=1, device_id={"blk": other}, device_id_type=MESH)

    own = [
        pltpu.make_async_copy(src, dst, local_sem.at[i])
        for i, (src, dst) in enumerate((
            (len_hbm, len_ref),
            (qreq_hbm, qreq_ref),
            (qoff_hbm, qoff_ref),
            (sreq_hbm, sreq_ref),
            (spos_hbm, spos_ref),
            (q_hbm, qs.at[0, :, pl.ds(0, QW)]),
            (k_hbm, ks.at[0]),
            (v_hbm, vs.at[0, :, pl.ds(0, HD)]),
        ))
    ]
    for copy in own:
        copy.start()
    for copy in own[:5]:
        copy.wait()

    request = qreq_ref[...]
    length = jnp.where(request == 0, len_ref[0], len_ref[1])
    position = length - 1 - qoff_ref[...]
    eye = lax.broadcasted_iota(jnp.int32, (TOK, TOK), 0) == lax.broadcasted_iota(jnp.int32, (TOK, TOK), 1)

    def column(row):
        return jnp.sum(jnp.where(eye, jnp.broadcast_to(row, (TOK, TOK)), 0), axis=1, keepdims=True)

    lane = lax.broadcasted_iota(jnp.int32, (TOK, HD), 1)
    position = column(position)
    meta = jnp.where(
        lane == 0, column(request),
        jnp.where(lane == 1, position // 128, jnp.where(lane == 2, position % 128, 0)),
    )
    qs[0, :, QW:] = meta.astype(F32).astype(BF16)
    code[0] = sreq_ref[...].astype(F32) * REQ_STEP + spos_ref[...].astype(F32)
    for copy in own[5:]:
        copy.wait()
    pl.semaphore_wait(barrier, 7)

    def remote(src, dst, send_sem, recv_sem, other):
        return pltpu.make_async_remote_copy(
            src_ref=src, dst_ref=dst, send_sem=send_sem, recv_sem=recv_sem,
            device_id={"blk": other}, device_id_type=MESH,
        )

    def kv_copies(chunk, src_slot, src_at, dst_slot, dst_at, other):
        src = pl.ds(src_at, HALF)
        dst = pl.ds(dst_at, HALF)
        return [
            remote(ks.at[src_slot, src], ks.at[dst_slot, dst],
                   kv_send.at[chunk, 0], kv_recv.at[chunk, 0], other),
            remote(vs.at[src_slot, src, pl.ds(0, HD)], vs.at[dst_slot, dst, pl.ds(0, HD)],
                   kv_send.at[chunk, 1], kv_recv.at[chunk, 1], other),
            remote(code.at[src_slot, :, src], code.at[dst_slot, :, dst],
                   kv_send.at[chunk, 2], kv_recv.at[chunk, 2], other),
        ]

    kv = [
        kv_copies(0, 0, HALF, 1, 0, right),
        kv_copies(1, 0, 0, 1, HALF, left),
        kv_copies(2, 0, 0, 2, 0, right),
        kv_copies(3, 0, HALF, 2, HALF, left),
        kv_copies(4, 1, 0, 3, HALF, right),
        kv_copies(5, 1, HALF, 3, 0, left),
    ]

    def q_copy(src_slot, dst_slot, begin, count, sem, other):
        rows = pl.ds(begin, count)
        return remote(qs.at[src_slot, rows], qs.at[dst_slot, rows], q_send.at[sem], q_recv.at[sem], other)

    q_low = q_copy(0, 7, 0, TOK, 7, up)
    q_high = q_copy(0, 1, 0, TOK, 1, down)
    q_far = q_copy(0, 4, 0, TOK, 4, far)
    q_low2 = q_copy(7, 6, 0, TOK, 6, up)
    q_high2 = q_copy(1, 2, 0, TOK, 2, down)
    q_low3 = q_copy(7, 5, 0, TOK, 5, up2)
    q_high3 = q_copy(1, 3, 0, TOK, 3, down2)
    qc = [q_low, q_high, q_far, q_low2, q_high2, q_low3, q_high3]

    def part_copies(src_slot, dst_slot, other):
        return [
            remote(sent.at[src_slot], got.at[dst_slot],
                   part_send.at[dst_slot, 0], part_recv.at[dst_slot, 0], other),
            remote(sent_stat.at[src_slot], got_stat.at[dst_slot],
                   part_send.at[dst_slot, 1], part_recv.at[dst_slot, 1], other),
        ]

    part = {
        1: part_copies(1, 0, up),
        7: part_copies(7, 1, down),
        2: part_copies(2, 2, up2),
        6: part_copies(6, 3, down2),
        4: part_copies(4, 4, far),
        3: part_copies(3, 5, up),
        5: part_copies(5, 6, down),
    }

    def start(copies):
        for copy in copies:
            copy.start()

    start([q_low, q_high])
    start(kv[0])
    start(kv[1])
    start([q_far])
    start(kv[2])
    start(kv[3])

    vs[:, :, HD:] = jnp.ones((NX, SLOT, HD), BF16)
    eye_hd = lax.broadcasted_iota(jnp.int32, (HD, HD), 0) == lax.broadcasted_iota(jnp.int32, (HD, HD), 1)

    def to_row(block):
        return jnp.sum(jnp.where(eye_hd, block, 0.0), axis=0, keepdims=True)

    def to_column(row):
        return jnp.sum(jnp.where(eye_hd, jnp.broadcast_to(row, (HD, HD)), 0.0), axis=1, keepdims=True)

    def state(query, g):
        rows = pl.ds(g * HD, HD)
        return peak[query, rows, :], acc[query, rows, 0:HD], acc[query, rows, HD:]

    def merge(mine, slot, g):
        rows = pl.ds(g * HD, HD)
        m, w, l = mine
        m_in = to_column(got_stat[slot, g, 0:1, :])
        l_in = to_column(got_stat[slot, g, 1:2, :])
        m_new = jnp.maximum(m, m_in)
        keep = jnp.exp2(m - m_new)
        take = jnp.exp2(m_in - m_new)
        return m_new, w * keep + got[slot, rows, :].astype(F32) * take, l * keep + l_in * take

    def finish(query):
        arrived = {2: (3, 5), 6: (5, 6)}.get(query)
        if arrived:
            for copy in part[arrived[0]]:
                copy.wait_recv()
        for g in range(4):
            now = state(query, g)
            if arrived:
                now = merge(now, arrived[1], g)
            m, w, l = now
            sent[query, pl.ds(g * HD, HD), :] = w.astype(BF16)
            sent_stat[query, g, 0:1, :] = to_row(m)
            sent_stat[query, g, 1:2, :] = to_row(l)
        start(part[query])

    actions = {}

    def at(stage, action):
        actions.setdefault(stage, []).append(action)

    def take_query(arriving, forward):
        def action():
            for copy in arriving:
                copy.wait_recv()
            start(forward)
        return action

    def take_keys(*chunks):
        def action():
            for chunk in chunks:
                kv[chunk][0].wait_recv()
                kv[chunk][2].wait_recv()
        return action

    def take_values(*chunks):
        def action():
            for chunk in chunks:
                kv[chunk][1].wait_recv()
        return action

    def send_on():
        start(kv[4])
        start(kv[5])

    at(first_use(0, 1) - 1, take_query([q_low, q_high], [q_low3, q_high3, q_low2, q_high2]))
    at(first_use(0, 2) - 1, take_query([q_low2, q_high2], []))
    at(first_use(0, 3) - 1, take_query([q_low3, q_high3], []))
    at(first_use(0, 4) - 1, take_query([q_far], []))
    for key, chunks in ((1, (0, 1)), (2, (2, 3)), (3, (4, 5))):
        at(first_use(1, key) - 1, take_keys(*chunks))
        at(first_use(1, key) + 1, take_values(*chunks))
    at(first_use(1, 1) + 1, send_on)
    for query in (3, 5, 4, 1, 7, 2, 6):
        at(last_use(query) + 2, functools.partial(finish, query))

    def scores(query, key, into):
        q = jnp.concatenate([qs[query, :, pl.ds(h * HD, HD)] for h in range(QH_DEV)], axis=0)
        into[...] = lax.dot_general(q, ks[key], (((1,), (1,)), ((), ())), preferred_element_type=F32)

    def mask(query, key, into):
        meta = qs[query, :, QW:].astype(F32)
        low = meta[:, 0:1] * REQ_STEP
        high = low + (meta[:, 1:2] * 128.0 + meta[:, 2:3])
        where = code[key]
        into[...] = jnp.where((where >= low) & (where <= high), 0.0, MASKED)

    def softmax(query, key, scored, masked, weights, shrink):
        bias = masked[...]
        for r in range(ROWS // SOFT_ROWS):
            rows = pl.ds(r * SOFT_ROWS, SOFT_ROWS)
            heads = SOFT_ROWS // TOK
            s = (scored[rows, :].reshape(heads, TOK, SLOT) * SCALE + bias[None]).reshape(SOFT_ROWS, SLOT)
            top = jnp.max(s, axis=1, keepdims=True)
            if key == 0:
                m_new = jnp.broadcast_to(jnp.maximum(top, FLOOR), (SOFT_ROWS, HD))
            else:
                m_old = peak[query, rows, :]
                m_new = jnp.maximum(m_old, top)
                shrink[rows, :] = jnp.exp2(m_old - m_new)
            weights[rows, :] = jnp.exp2(s - m_new[:, 0:1]).astype(BF16)
            peak[query, rows, :] = m_new

    def values(query, key, weights, shrink):
        o = jnp.dot(weights[...], vs[key], preferred_element_type=F32)
        if key == 0:
            acc[query] = o
        else:
            keep = shrink[...]
            acc[query, :, 0:HD] = acc[query, :, 0:HD] * keep + o[:, 0:HD]
            acc[query, :, HD:] = acc[query, :, HD:] * keep + o[:, HD:]

    scores(*PAIRS[0], s0)
    mask(*PAIRS[0], b0)
    buffers = ((s0, b0, p0, a0), (s1, b1, p1, a1))
    for i in range(N):
        for action in actions.get(i, ()):
            action()
        (s_now, b_now, p_now, a_now), (s_next, b_next, p_last, a_last) = buffers[i % 2], buffers[1 - i % 2]
        if i + 1 < N:
            scores(*PAIRS[i + 1], s_next)
            mask(*PAIRS[i + 1], b_next)
        softmax(*PAIRS[i], s_now, b_now, p_now, a_now)
        if i:
            values(*PAIRS[i - 1], p_last, a_last)
    values(*PAIRS[N - 1], p1, a1)

    for query in (4, 2, 6, 1, 7):
        for copy in part[query]:
            copy.wait_recv()
    for g in range(4):
        now = state(0, g)
        for slot in range(5):
            now = merge(now, slot, g)
        o = (now[1] / now[2]).astype(BF16)
        for h in range(4):
            out_ref[:, pl.ds((g * 4 + h) * HD, HD)] = o[h * TOK:(h + 1) * TOK, :]

    for copies in kv:
        for copy in copies:
            copy.wait_send()
    for copy in qc:
        copy.wait_send()
    for copies in part.values():
        for copy in copies:
            copy.wait_send()


def shards(
    queries,
    cache_keys,
    cache_values,
    slot_request,
    slot_position,
    lengths,
    query_request,
    query_offset,
):
    vmem = pl.BlockSpec(memory_space=pltpu.VMEM)
    hbm = pl.BlockSpec(memory_space=pltpu.HBM)
    dma = pltpu.SemaphoreType.DMA
    return pl.pallas_call(
        kernel,
        out_shape=jax.ShapeDtypeStruct((TOK, QW), BF16),
        in_specs=[hbm] * 8,
        out_specs=vmem,
        scratch_shapes=[
            pltpu.SMEM((2,), jnp.int32),
            pltpu.VMEM((1, TOK), jnp.int32),
            pltpu.VMEM((1, TOK), jnp.int32),
            pltpu.VMEM((1, SLOT), jnp.int32),
            pltpu.VMEM((1, SLOT), jnp.int32),
            pltpu.VMEM((NZ, TOK, QW + HD), BF16),
            pltpu.VMEM((NX, SLOT, HD), BF16),
            pltpu.VMEM((NX, SLOT, 2 * HD), BF16),
            pltpu.VMEM((NX, 1, SLOT), F32),
            pltpu.VMEM((TOK, SLOT), F32),
            pltpu.VMEM((TOK, SLOT), F32),
            pltpu.VMEM((ROWS, SLOT), F32),
            pltpu.VMEM((ROWS, SLOT), F32),
            pltpu.VMEM((ROWS, SLOT), BF16),
            pltpu.VMEM((ROWS, SLOT), BF16),
            pltpu.VMEM((ROWS, HD), F32),
            pltpu.VMEM((ROWS, HD), F32),
            pltpu.VMEM((NZ, ROWS, 2 * HD), F32),
            pltpu.VMEM((NZ, ROWS, HD), F32),
            pltpu.VMEM((NZ, ROWS, HD), BF16),
            pltpu.VMEM((NZ, 4, 8, HD), F32),
            pltpu.VMEM((NZ, ROWS, HD), BF16),
            pltpu.VMEM((NZ, 4, 8, HD), F32),
            dma((8,)),
            dma((6, 3)),
            dma((6, 3)),
            dma((NZ,)),
            dma((NZ,)),
            dma((NZ, 2)),
            dma((NZ, 2)),
        ],
        compiler_params=pltpu.CompilerParams(
            collective_id=0, has_side_effects=True, vmem_limit_bytes=63 * 2 ** 20
        ),
        cost_estimate=pl.CostEstimate(
            flops=4 * ROWS * SLOT * HD * N, bytes_accessed=2 ** 20, transcendentals=ROWS * SLOT * N
        ),
        name="ring_attention",
    )(
        lengths,
        query_request.reshape(1, TOK),
        query_offset.reshape(1, TOK),
        slot_request.reshape(1, SLOT),
        slot_position.reshape(1, SLOT),
        queries,
        cache_keys,
        cache_values,
    )


def solution(mesh):
    return jax.shard_map(
        shards,
        mesh=mesh,
        in_specs=(
            P(("rep", "blk"), "head"),
            P(("rep", "blk"), "head"),
            P(("rep", "blk"), "head"),
            P(("rep", "blk")),
            P(("rep", "blk")),
            P("rep"),
            P(("rep", "blk")),
            P(("rep", "blk")),
        ),
        out_specs=P(("rep", "blk"), "head"),
        check_vma=False,
    )
```

time: 63.7 us -> 58.1 us (0.912)
  local copies, waits for them, and re-layouts: 4.84 us -> 1.57 us
  Pallas kernels: 58.6 us -> 56.4 us
    unnamed x17 -> x1, local copies, waits for them, and re-layouts: 4.84 us -> 1.57 us
    pallas_call x1, Pallas kernels: 58.6 us -> 56.4 us  [shards(): pl.pallas_call(kernel, out_shape=jax.ShapeDtypeStruct((TOK, QW), BF16), i...]
where the time goes in v2:
time: 58.1 us; the launch traced here: 58 us
  Pallas kernels  56.4 us (97%)
  local copies, waits for them, and re-layouts  1.57 us (3%)
    pallas_call x1, Pallas kernels, shards(): pl.pallas_call(kernel, out_shape=jax.ShapeDtypeStruct((TOK, QW), BF16), i...  56.4 us
    unnamed x1, local copies, waits for them, and re-layouts  1.57 us

profile of v2, /device:TPU:16, one launch (start us, length us, event | category | flops | bytes accessed | tf_op | source)
XLA Modules:
  0.0 58.0 jit_solution(4383090454006476454)
XLA Ops:
  0.0 56.4 %ring_attention.1 = bf16[32,2048]{1,0:T(8,128)(2,1)} custom-call(s32[2]{0:T(128)} %len_hbm.1, s32[1,32]{1,0:T(1,128)} %bitcast.6, s32[1,32]{1,0:T(1,128)} %bitcast.7, s32[1,1024]{1,0:T(1,128)} %bitcast.4, s32[1,1024]{1,0:T(1,128)} %bitcast.5, bf16[32,2048]{1,0:T(8,128)(2,1)} %q_hbm.1, bf16[1024,128]{1,0:T(8,128)(2,1)} %k_hbm.1, bf16[1024,128]{1,0:T(8,128)(2,1)} %v_hbm.1), custom_call_target="tpu_custom_call" | custom-call | flops 8589934592 | bytes 1048576 | tf_op jit(solution)/shard_map/ring_attention/pallas_call | solution.py:338
  56.4 1.6 %copy.10 = bf16[32,2048]{1,0:T(8,128)(2,1)} copy(bf16[32,2048]{1,0:T(8,128)(2,1)} %ring_attention.1) | data formatting | bytes 262144

commit v3 on v2

v3 whole, which is shorter than its diff:
```python
import functools

import jax
import jax.numpy as jnp
from jax import lax
from jax.experimental import pallas as pl
from jax.experimental.pallas import tpu as pltpu
from jax.sharding import PartitionSpec as P

HD = 128
QH_DEV = 16
TOK = 32
ROWS = TOK * QH_DEV
SLOT = 1024
HALF = SLOT // 2
QW = QH_DEV * HD
NZ = 8
NX = 4
SCALE = 1.4426950408889634 * HD ** -0.5
MASKED = -1e30
FLOOR = -1e29
REQ_STEP = 65536.0
SOFT_ROWS = 128
MESH = pl.DeviceIdType.MESH
F32 = jnp.float32
BF16 = jnp.bfloat16

PAIRS = (
    (0, 0), (1, 0), (7, 0), (1, 1), (7, 1), (0, 1), (3, 0), (5, 0),
    (3, 1), (5, 1), (3, 2), (5, 2), (4, 0), (4, 1), (4, 2), (3, 3),
    (5, 3), (4, 3), (2, 0), (6, 0), (2, 1), (6, 1), (2, 2), (6, 2),
    (2, 3), (6, 3), (1, 2), (1, 3), (7, 2), (7, 3), (0, 2), (0, 3),
)
N = len(PAIRS)


def first_use(kind, value):
    return min(i for i, pair in enumerate(PAIRS) if pair[kind] == value)


def last_use(query):
    return max(i for i, pair in enumerate(PAIRS) if pair[0] == query)


def kernel(
    len_hbm, qreq_hbm, qoff_hbm, sreq_hbm, spos_hbm, q_hbm, k_hbm, v_hbm,
    out_ref,
    len_ref, qreq_ref, qoff_ref, sreq_ref, spos_ref,
    qs, ks, vs, code, b0, b1, s0, s1, p0, p1, a0, a1, acc, peak,
    sent, sent_stat, got, got_stat,
    local_sem, kv_send, kv_recv, q_send, q_recv, part_send, part_recv,
):
    me = lax.axis_index("blk")
    z = me // NX
    x = lax.rem(me, NX)

    def along_z(step):
        return lax.rem(z + step + NZ, NZ) * NX + x

    right = z * NX + lax.rem(x + 1, NX)
    left = z * NX + lax.rem(x + NX - 1, NX)
    up, up2, down2, down = (along_z(step) for step in (1, 2, -2, -1))

    barrier = pltpu.get_barrier_semaphore()
    for other in (up, down, right, left, up2, down2):
        pl.semaphore_signal(barrier, inc=1, device_id={"blk": other}, device_id_type=MESH)

    own = [
        pltpu.make_async_copy(src, dst, local_sem.at[i])
        for i, (src, dst) in enumerate((
            (len_hbm, len_ref),
            (qreq_hbm, qreq_ref),
            (qoff_hbm, qoff_ref),
            (sreq_hbm, sreq_ref),
            (spos_hbm, spos_ref),
            (q_hbm, qs.at[0, :, pl.ds(0, QW)]),
            (k_hbm, ks.at[0]),
            (v_hbm, vs.at[0]),
        ))
    ]
    for copy in own:
        copy.start()
    for copy in own[:5]:
        copy.wait()

    request = qreq_ref[...]
    length = jnp.where(request == 0, len_ref[0], len_ref[1])
    position = length - 1 - qoff_ref[...]
    eye = lax.broadcasted_iota(jnp.int32, (TOK, TOK), 0) == lax.broadcasted_iota(jnp.int32, (TOK, TOK), 1)

    def column(row):
        return jnp.sum(jnp.where(eye, jnp.broadcast_to(row, (TOK, TOK)), 0), axis=1, keepdims=True)

    lane = lax.broadcasted_iota(jnp.int32, (TOK, HD), 1)
    position = column(position)
    meta = jnp.where(
        lane == 0, column(request),
        jnp.where(lane == 1, position // 128, jnp.where(lane == 2, position % 128, 0)),
    )
    qs[0, :, QW:] = meta.astype(F32).astype(BF16)
    code[0] = sreq_ref[...].astype(F32) * REQ_STEP + spos_ref[...].astype(F32)
    def scores(query, key, into):
        q = jnp.concatenate([qs[query, :, pl.ds(h * HD, HD)] for h in range(QH_DEV)], axis=0)
        into[...] = lax.dot_general(q, ks[key], (((1,), (1,)), ((), ())), preferred_element_type=F32)

    def mask(query, key, into):
        meta = qs[query, :, QW:].astype(F32)
        low = meta[:, 0:1] * REQ_STEP
        high = low + (meta[:, 1:2] * 128.0 + meta[:, 2:3])
        where = code[key]
        into[...] = jnp.where((where >= low) & (where <= high), 0.0, MASKED)

    def softmax(query, key, scored, masked, weights, shrink):
        bias = masked[...]
        for r in range(ROWS // SOFT_ROWS):
            rows = pl.ds(r * SOFT_ROWS, SOFT_ROWS)
            heads = SOFT_ROWS // TOK
            s = (scored[rows, :].reshape(heads, TOK, SLOT) * SCALE + bias[None]).reshape(SOFT_ROWS, SLOT)
            top = jnp.max(s, axis=1, keepdims=True)
            if key == 0:
                m_new = jnp.broadcast_to(jnp.maximum(top, FLOOR), (SOFT_ROWS, HD))
            else:
                m_old = peak[query, rows, :]
                m_new = jnp.maximum(m_old, top)
                shrink[rows, :] = jnp.exp2(m_old - m_new)
            weights[rows, :] = jnp.exp2(s - m_new[:, 0:1]).astype(BF16)
            peak[query, rows, :] = m_new

    def values(query, key, weights, shrink):
        columns = jnp.concatenate([vs[key], jnp.ones((SLOT, HD), BF16)], axis=1)
        o = jnp.dot(weights[...], columns, preferred_element_type=F32)
        if key == 0:
            acc[query] = o
        else:
            keep = shrink[...]
            acc[query, :, 0:HD] = acc[query, :, 0:HD] * keep + o[:, 0:HD]
            acc[query, :, HD:] = acc[query, :, HD:] * keep + o[:, HD:]

    for copy in own[5:]:
        copy.wait()
    scores(*PAIRS[0], s0)
    mask(*PAIRS[0], b0)
    softmax(*PAIRS[0], s0, b0, p0, a0)
    pl.semaphore_wait(barrier, 6)

    def remote(src, dst, send_sem, recv_sem, other):
        return pltpu.make_async_remote_copy(
            src_ref=src, dst_ref=dst, send_sem=send_sem, recv_sem=recv_sem,
            device_id={"blk": other}, device_id_type=MESH,
        )

    def kv_copies(chunk, src_slot, src_at, dst_slot, dst_at, other):
        src = pl.ds(src_at, HALF)
        dst = pl.ds(dst_at, HALF)
        return [
            remote(ks.at[src_slot, src], ks.at[dst_slot, dst],
                   kv_send.at[chunk, 0], kv_recv.at[chunk, 0], other),
            remote(vs.at[src_slot, src], vs.at[dst_slot, dst],
                   kv_send.at[chunk, 1], kv_recv.at[chunk, 1], other),
            remote(code.at[src_slot, :, src], code.at[dst_slot, :, dst],
                   kv_send.at[chunk, 2], kv_recv.at[chunk, 2], other),
        ]

    kv = [
        kv_copies(0, 0, HALF, 1, 0, right),
        kv_copies(1, 0, 0, 1, HALF, left),
        kv_copies(2, 0, 0, 2, 0, right),
        kv_copies(3, 0, HALF, 2, HALF, left),
        kv_copies(4, 1, 0, 3, HALF, right),
        kv_copies(5, 1, HALF, 3, 0, left),
    ]

    def q_copy(src_slot, dst_slot, begin, count, sem, other):
        rows = pl.ds(begin, count)
        return remote(qs.at[src_slot, rows], qs.at[dst_slot, rows], q_send.at[sem], q_recv.at[sem], other)

    q_low = q_copy(0, 7, 0, TOK, 7, up)
    q_high = q_copy(0, 1, 0, TOK, 1, down)
    q_low3 = q_copy(7, 5, 0, TOK, 5, up2)
    q_high3 = q_copy(1, 3, 0, TOK, 3, down2)
    q_low2 = q_copy(7, 6, 0, TOK, 6, up)
    q_high2 = q_copy(1, 2, 0, TOK, 2, down)
    q_low4 = q_copy(5, 4, 0, TOK // 2, 4, up)
    q_high4 = q_copy(3, 4, TOK // 2, TOK // 2, 0, down)
    qc = [q_low, q_high, q_low3, q_high3, q_low2, q_high2, q_low4, q_high4]

    def part_copies(src_slot, dst_slot, other, begin=0, count=ROWS):
        rows = pl.ds(begin, count)
        stats = pl.ds(begin // HD, count // HD)
        return [
            remote(sent.at[src_slot, rows], got.at[dst_slot, rows],
                   part_send.at[dst_slot, 0], part_recv.at[dst_slot, 0], other),
            remote(sent_stat.at[src_slot, stats], got_stat.at[dst_slot, stats],
                   part_send.at[dst_slot, 1], part_recv.at[dst_slot, 1], other),
        ]

    part = {
        1: {0: part_copies(1, 0, up)},
        7: {1: part_copies(7, 1, down)},
        2: {2: part_copies(2, 2, up2)},
        6: {3: part_copies(6, 3, down2)},
        3: {5: part_copies(3, 5, up)},
        5: {6: part_copies(5, 6, down)},
        4: {4: part_copies(4, 4, up2, 0, ROWS // 2),
            7: part_copies(4, 7, down2, ROWS // 2, ROWS // 2)},
    }
    parts = {slot: copies for slots in part.values() for slot, copies in slots.items()}

    def start(copies):
        for copy in copies:
            copy.start()

    start([q_low, q_high])
    start(kv[0])
    start(kv[1])

    eye_hd = lax.broadcasted_iota(jnp.int32, (HD, HD), 0) == lax.broadcasted_iota(jnp.int32, (HD, HD), 1)

    def to_row(block):
        return jnp.sum(jnp.where(eye_hd, block, 0.0), axis=0, keepdims=True)

    def to_column(row):
        return jnp.sum(jnp.where(eye_hd, jnp.broadcast_to(row, (HD, HD)), 0.0), axis=1, keepdims=True)

    def state(query, g):
        rows = pl.ds(g * HD, HD)
        return peak[query, rows, :], acc[query, rows, 0:HD], acc[query, rows, HD:]

    def merge(mine, slot, g):
        rows = pl.ds(g * HD, HD)
        m, w, l = mine
        m_in = to_column(got_stat[slot, g, 0:1, :])
        l_in = to_column(got_stat[slot, g, 1:2, :])
        m_new = jnp.maximum(m, m_in)
        keep = jnp.exp2(m - m_new)
        take = jnp.exp2(m_in - m_new)
        return m_new, w * keep + got[slot, rows, :].astype(F32) * take, l * keep + l_in * take

    def finish(query):
        arrived = {2: {5: (0, 1, 2, 3), 4: (0, 1)}, 6: {6: (0, 1, 2, 3), 7: (2, 3)}}.get(query, {})
        for slot in arrived:
            for copy in parts[slot]:
                copy.wait_recv()
        for g in range(4):
            now = state(query, g)
            for slot, groups in arrived.items():
                if g in groups:
                    now = merge(now, slot, g)
            m, w, l = now
            sent[query, pl.ds(g * HD, HD), :] = w.astype(BF16)
            sent_stat[query, g, 0:1, :] = to_row(m)
            sent_stat[query, g, 1:2, :] = to_row(l)
        for copies in part[query].values():
            start(copies)

    actions = {}

    def at(stage, action):
        actions.setdefault(stage, []).append(action)

    def take_queries(*arriving):
        for copy in arriving:
            copy.wait_recv()

    def take_keys(*chunks):
        for chunk in chunks:
            for copy in kv[chunk]:
                copy.wait_recv()

    at(first_use(0, 1) - 1, lambda: take_queries(q_low, q_high))
    at(first_use(0, 1) - 1, lambda: start([q_low3, q_high3] + kv[2] + kv[3]))
    at(first_use(1, 1) - 1, lambda: take_keys(0, 1))
    at(first_use(1, 1) - 1, lambda: start(kv[4] + kv[5]))
    at(first_use(0, 3) - 1, lambda: take_queries(q_low3, q_high3))
    at(first_use(0, 3) - 1, lambda: start([q_low2, q_high2, q_low4, q_high4]))
    at(first_use(1, 2) - 1, lambda: take_keys(2, 3))
    at(first_use(0, 4) - 1, lambda: take_queries(q_low4, q_high4))
    at(first_use(1, 3) - 1, lambda: take_keys(4, 5))
    at(first_use(0, 2) - 1, lambda: take_queries(q_low2, q_high2))
    for query in (3, 5, 4, 2, 6, 1, 7):
        at(last_use(query) + 2 + (query == 3), functools.partial(finish, query))

    buffers = ((s0, b0, p0, a0), (s1, b1, p1, a1))
    for i in range(N):
        for action in actions.get(i, ()):
            action()
        (s_now, b_now, p_now, a_now), (s_next, b_next, p_last, a_last) = buffers[i % 2], buffers[1 - i % 2]
        if i + 1 < N:
            scores(*PAIRS[i + 1], s_next)
            mask(*PAIRS[i + 1], b_next)
        if i:
            softmax(*PAIRS[i], s_now, b_now, p_now, a_now)
            values(*PAIRS[i - 1], p_last, a_last)
    values(*PAIRS[N - 1], p1, a1)

    for slot in range(4):
        for copy in parts[slot]:
            copy.wait_recv()
    for g in range(4):
        now = state(0, g)
        for slot in range(4):
            now = merge(now, slot, g)
        o = (now[1] / now[2]).astype(BF16)
        for h in range(4):
            out_ref[:, pl.ds((g * 4 + h) * HD, HD)] = o[h * TOK:(h + 1) * TOK, :]

    for copies in kv:
        for copy in copies:
            copy.wait_send()
    for copy in qc:
        copy.wait_send()
    for copies in parts.values():
        for copy in copies:
            copy.wait_send()


def shards(
    queries,
    cache_keys,
    cache_values,
    slot_request,
    slot_position,
    lengths,
    query_request,
    query_offset,
):
    vmem = pl.BlockSpec(memory_space=pltpu.VMEM)
    hbm = pl.BlockSpec(memory_space=pltpu.HBM)
    dma = pltpu.SemaphoreType.DMA
    return pl.pallas_call(
        kernel,
        out_shape=jax.ShapeDtypeStruct((TOK, QW), BF16),
        in_specs=[hbm] * 8,
        out_specs=vmem,
        scratch_shapes=[
            pltpu.SMEM((2,), jnp.int32),
            pltpu.VMEM((1, TOK), jnp.int32),
            pltpu.VMEM((1, TOK), jnp.int32),
            pltpu.VMEM((1, SLOT), jnp.int32),
            pltpu.VMEM((1, SLOT), jnp.int32),
            pltpu.VMEM((NZ, TOK, QW + HD), BF16),
            pltpu.VMEM((NX, SLOT, HD), BF16),
            pltpu.VMEM((NX, SLOT, HD), BF16),
            pltpu.VMEM((NX, 1, SLOT), F32),
            pltpu.VMEM((TOK, SLOT), F32),
            pltpu.VMEM((TOK, SLOT), F32),
            pltpu.VMEM((ROWS, SLOT), F32),
            pltpu.VMEM((ROWS, SLOT), F32),
            pltpu.VMEM((ROWS, SLOT), BF16),
            pltpu.VMEM((ROWS, SLOT), BF16),
            pltpu.VMEM((ROWS, HD), F32),
            pltpu.VMEM((ROWS, HD), F32),
            pltpu.VMEM((NZ, ROWS, 2 * HD), F32),
            pltpu.VMEM((NZ, ROWS, HD), F32),
            pltpu.VMEM((NZ, ROWS, HD), BF16),
            pltpu.VMEM((NZ, 4, 8, HD), F32),
            pltpu.VMEM((NZ, ROWS, HD), BF16),
            pltpu.VMEM((NZ, 4, 8, HD), F32),
            dma((8,)),
            dma((6, 3)),
            dma((6, 3)),
            dma((NZ,)),
            dma((NZ,)),
            dma((NZ, 2)),
            dma((NZ, 2)),
        ],
        compiler_params=pltpu.CompilerParams(
            collective_id=0, has_side_effects=True, vmem_limit_bytes=63 * 2 ** 20
        ),
        cost_estimate=pl.CostEstimate(
            flops=4 * ROWS * SLOT * HD * N, bytes_accessed=2 ** 20, transcendentals=ROWS * SLOT * N
        ),
        name="ring_attention",
    )(
        lengths,
        query_request.reshape(1, TOK),
        query_offset.reshape(1, TOK),
        slot_request.reshape(1, SLOT),
        slot_position.reshape(1, SLOT),
        queries,
        cache_keys,
        cache_values,
    )


def solution(mesh):
    return jax.shard_map(
        shards,
        mesh=mesh,
        in_specs=(
            P(("rep", "blk"), "head"),
            P(("rep", "blk"), "head"),
            P(("rep", "blk"), "head"),
            P(("rep", "blk")),
            P(("rep", "blk")),
            P("rep"),
            P(("rep", "blk")),
            P(("rep", "blk")),
        ),
        out_specs=P(("rep", "blk"), "head"),
        check_vma=False,
    )
```

time: 58.1 us -> 52.9 us (0.910)
  Pallas kernels: 56.4 us -> 51.2 us
    pallas_call x1, Pallas kernels: 56.4 us -> 51.2 us  [shards(): pl.pallas_call(kernel, out_shape=jax.ShapeDtypeStruct((TOK, QW), BF16), i...]
where the time goes in v3:
time: 52.9 us; the launch traced here: 52.8 us
  Pallas kernels  51.2 us (97%)
  local copies, waits for them, and re-layouts  1.57 us (3%)
    pallas_call x1, Pallas kernels, shards(): pl.pallas_call(kernel, out_shape=jax.ShapeDtypeStruct((TOK, QW), BF16), i...  51.2 us
    unnamed x1, local copies, waits for them, and re-layouts  1.57 us

profile of v3, /device:TPU:16, one launch (start us, length us, event | category | flops | bytes accessed | tf_op | source)
XLA Modules:
  0.0 52.8 jit_solution(6175218735114668940)
XLA Ops:
  0.0 51.2 %ring_attention.1 = bf16[32,2048]{1,0:T(8,128)(2,1)} custom-call(s32[2]{0:T(128)} %len_hbm.1, s32[1,32]{1,0:T(1,128)} %bitcast.6, s32[1,32]{1,0:T(1,128)} %bitcast.7, s32[1,1024]{1,0:T(1,128)} %bitcast.4, s32[1,1024]{1,0:T(1,128)} %bitcast.5, bf16[32,2048]{1,0:T(8,128)(2,1)} %q_hbm.1, bf16[1024,128]{1,0:T(8,128)(2,1)} %k_hbm.1, bf16[1024,128]{1,0:T(8,128)(2,1)} %v_hbm.1), custom_call_target="tpu_custom_call" | custom-call | flops 8589934592 | bytes 1048576 | tf_op jit(solution)/shard_map/ring_attention/pallas_call | solution.py:330
  51.2 1.6 %copy.10 = bf16[32,2048]{1,0:T(8,128)(2,1)} copy(bf16[32,2048]{1,0:T(8,128)(2,1)} %ring_attention.1) | data formatting | bytes 262144

commit v4 on v3

--- a/solution.py
+++ b/solution.py
@@ -32,6 +32,8 @@
     (2, 3), (6, 3), (1, 2), (1, 3), (7, 2), (7, 3), (0, 2), (0, 3),
 )
 N = len(PAIRS)
+FINISH = ((3, 18), (5, 18), (4, 19), (2, 26), (6, 27), (1, 29), (7, 31))
+ARRIVALS = (2, 3, 0, 1)
 
 
 def first_use(kind, value):
@@ -211,8 +213,8 @@
             copy.start()
 
     start([q_low, q_high])
-    start(kv[0])
-    start(kv[1])
+    for part_of in (0, 2, 1):
+        start([kv[0][part_of], kv[1][part_of]])
 
     eye_hd = lax.broadcasted_iota(jnp.int32, (HD, HD), 0) == lax.broadcasted_iota(jnp.int32, (HD, HD), 1)
 
@@ -264,21 +266,31 @@
 
     def take_keys(*chunks):
         for chunk in chunks:
-            for copy in kv[chunk]:
-                copy.wait_recv()
+            kv[chunk][0].wait_recv()
+            kv[chunk][2].wait_recv()
+
+    def take_values(*chunks):
+        for chunk in chunks:
+            kv[chunk][1].wait_recv()
 
     at(first_use(0, 1) - 1, lambda: take_queries(q_low, q_high))
-    at(first_use(0, 1) - 1, lambda: start([q_low3, q_high3] + kv[2] + kv[3]))
+    at(first_use(0, 1) - 1, lambda: start(
+        [q_low3, q_high3] + [kv[chunk][part_of] for part_of in (0, 2, 1) for chunk in (2, 3)]
+    ))
     at(first_use(1, 1) - 1, lambda: take_keys(0, 1))
-    at(first_use(1, 1) - 1, lambda: start(kv[4] + kv[5]))
+    at(first_use(1, 1) - 1, lambda: start([kv[4][0], kv[4][2], kv[5][0], kv[5][2]]))
+    at(first_use(1, 1) + 1, lambda: take_values(0, 1))
+    at(first_use(1, 1) + 1, lambda: start([kv[4][1], kv[5][1]]))
     at(first_use(0, 3) - 1, lambda: take_queries(q_low3, q_high3))
     at(first_use(0, 3) - 1, lambda: start([q_low2, q_high2, q_low4, q_high4]))
     at(first_use(1, 2) - 1, lambda: take_keys(2, 3))
+    at(first_use(1, 2) + 1, lambda: take_values(2, 3))
     at(first_use(0, 4) - 1, lambda: take_queries(q_low4, q_high4))
     at(first_use(1, 3) - 1, lambda: take_keys(4, 5))
-    at(first_use(0, 2) - 1, lambda: take_queries(q_low2, q_high2))
-    for query in (3, 5, 4, 2, 6, 1, 7):
-        at(last_use(query) + 2 + (query == 3), functools.partial(finish, query))
+    at(first_use(1, 3) + 1, lambda: take_values(4, 5))
+    at(first_use(0, 2) - 2, lambda: take_queries(q_low2, q_high2))
+    for query, stage in FINISH:
+        at(stage, functools.partial(finish, query))
 
     buffers = ((s0, b0, p0, a0), (s1, b1, p1, a1))
     for i in range(N):
@@ -293,16 +305,20 @@
             values(*PAIRS[i - 1], p_last, a_last)
     values(*PAIRS[N - 1], p1, a1)
 
-    for slot in range(4):
+    for slot in ARRIVALS:
         for copy in parts[slot]:
             copy.wait_recv()
-    for g in range(4):
-        now = state(0, g)
-        for slot in range(4):
-            now = merge(now, slot, g)
-        o = (now[1] / now[2]).astype(BF16)
-        for h in range(4):
-            out_ref[:, pl.ds((g * 4 + h) * HD, HD)] = o[h * TOK:(h + 1) * TOK, :]
+        for g in range(4):
+            m, w, l = merge(state(0, g), slot, g)
+            rows = pl.ds(g * HD, HD)
+            if slot != ARRIVALS[-1]:
+                peak[0, rows, :] = m
+                acc[0, rows, 0:HD] = w
+                acc[0, rows, HD:] = l
+                continue
+            o = (w / l).astype(BF16)
+            for h in range(4):
+                out_ref[:, pl.ds((g * 4 + h) * HD, HD)] = o[h * TOK:(h + 1) * TOK, :]
 
     for copies in kv:
         for copy in copies:

time: 52.9 us -> 50.9 us (0.962)
  Pallas kernels: 51.2 us -> 49.2 us
    pallas_call x1, Pallas kernels: 51.2 us -> 49.2 us  [shards(): pl.pallas_call(kernel, out_shape=jax.ShapeDtypeStruct((TOK, QW), BF16), i...]
where the time goes in v4:
time: 50.9 us; the launch traced here: 50.8 us
  Pallas kernels  49.2 us (97%)
  local copies, waits for them, and re-layouts  1.57 us (3%)
    pallas_call x1, Pallas kernels, shards(): pl.pallas_call(kernel, out_shape=jax.ShapeDtypeStruct((TOK, QW), BF16), i...  49.2 us
    unnamed x1, local copies, waits for them, and re-layouts  1.57 us

profile of v4, /device:TPU:16, one launch (start us, length us, event | category | flops | bytes accessed | tf_op | source)
XLA Modules:
  0.0 50.8 jit_solution(17698451343410040747)
XLA Ops:
  0.0 49.2 %ring_attention.1 = bf16[32,2048]{1,0:T(8,128)(2,1)} custom-call(s32[2]{0:T(128)} %len_hbm.1, s32[1,32]{1,0:T(1,128)} %bitcast.6, s32[1,32]{1,0:T(1,128)} %bitcast.7, s32[1,1024]{1,0:T(1,128)} %bitcast.4, s32[1,1024]{1,0:T(1,128)} %bitcast.5, bf16[32,2048]{1,0:T(8,128)(2,1)} %q_hbm.1, bf16[1024,128]{1,0:T(8,128)(2,1)} %k_hbm.1, bf16[1024,128]{1,0:T(8,128)(2,1)} %v_hbm.1), custom_call_target="tpu_custom_call" | custom-call | flops 8589934592 | bytes 1048576 | tf_op jit(solution)/shard_map/ring_attention/pallas_call | solution.py:346
  49.2 1.6 %copy.10 = bf16[32,2048]{1,0:T(8,128)(2,1)} copy(bf16[32,2048]{1,0:T(8,128)(2,1)} %ring_attention.1) | data formatting | bytes 262144
